TPU v7x, 32 devices: a whole 2x2x4 slice. The times are simulated.
32 devices in a mesh: cuts: 2 (over core), tile: 16 (over z, y, x).
Axes of the slice: x: 2, y: 2, z: 4, core: 2. Of those that a mesh axis runs over, the one named last changes fastest.
Arguments:
- object_slices: float32 [2, 2, 2048, 2048], P('cuts', None, 'tile'), may hold values from -1 to 1, as said below
- probe: float32 [2, 256, 256], replicated, may hold values from -4 to 4
- positions: int32 [32, 2], P('tile'), may hold values from 0 to 1792, as said below
- counts: int32 [16], P('tile'), may hold values from 1 to 2
- intensity: float32 [32, 256, 256], P('tile'), may hold values from 0 to 2
Outputs:
- object_grad: float32 [2, 2, 2048, 2048], P('cuts', None, 'tile')
Inputs may be any that keep to these rules, and one draw needn't show every extreme that they name: `positions`: slot s belongs to strip t = s // 2; its row offset lies between max(0, (t - 1) * 128) and min(t * 128, 1792), its column offset between 0 and 1792. `object_slices`: every object cell has a magnitude between 0.7 and 1.0.
All inputs are finite; a program needn't handle non-finite values.
Results may differ from a plain program's by a relative error of at most 0.00015.
Values sent between devices are 32-bit elements; how exact they have to be, the bound alone decides.
A program may use at most 64 MiB of HBM per device.

v0:
```python
import functools
import math

import jax
import jax.numpy as jnp
import ml_dtypes
import numpy as np
from jax import lax
from jax.experimental import pallas as pl
from jax.experimental.pallas import tpu as pltpu
from jax.sharding import PartitionSpec as P

MESH = pl.DeviceIdType.MESH
LANES = 128


def split_table(table):
    high = table.astype(ml_dtypes.bfloat16)
    low = (table - high.astype(np.float64)).astype(ml_dtypes.bfloat16)
    return np.stack([high, low])


def build_tables(window):
    counter = np.arange(window)
    turned = (counter[:, None] * counter[None, :] % window) * (2.0 * math.pi / window)
    dft = np.exp(-1j * turned) / math.sqrt(window)
    centred = (counter + window // 2) % window - window // 2
    angle = (centred * centred % (4 * window)) * (math.pi / (2 * window))
    prop = (np.conj(dft) * np.exp(-1j * angle)[None, :]) @ dft

    def right(matrix):
        return np.block([[matrix.real, matrix.imag], [-matrix.imag, matrix.real]])

    return np.stack(
        [split_table(m) for w in (dft, prop) for m in (right(w), right(w).T)]
    )


def halves(value):
    high = value.astype(jnp.bfloat16)
    return high, (value - high.astype(jnp.float32)).astype(jnp.bfloat16)


def dot(left, right):
    return jnp.dot(left, right, preferred_element_type=jnp.float32)


def sandwich(real_in, imag_in, table, right, left):
    window = real_in.shape[0]
    high, low = halves(jnp.concatenate([real_in, imag_in], axis=1))
    middle = dot(high, table[right, 0]) + (dot(low, table[right, 0]) + dot(high, table[right, 1]))
    stacked = jnp.concatenate([middle[:, :window], middle[:, window:]], axis=0)
    high, low = halves(stacked)
    final = dot(table[left, 0], high) + (dot(table[left, 0], low) + dot(table[left, 1], high))
    return final[:window], final[window:]


def roll_kernel(rows, pos, probe, rolled):
    core = lax.axis_index("cuts")
    window = probe.shape[1]
    row = jnp.where(core == 0, pos[0, 0], pos[1, 0]) - (lax.axis_index("tile") - 1) * rows
    row = jnp.clip(row, 0, rows)
    turn = jnp.clip(jnp.where(core == 0, pos[0, 1], pos[1, 1]), 0) % window
    for part in range(2):
        rolled[part] = pltpu.roll(pltpu.roll(probe[part], row, 0), turn, 1)


def cut_kernel(strip, starts, cut):
    blocks = strip.shape[2] // LANES
    lane_row = lax.broadcasted_iota(jnp.int32, (1, LANES), 1)
    for item in range(6):
        start = jnp.full((1, LANES), starts[item], jnp.int32)
        for half in range(2):
            order = list(range(half, blocks, 2))[::-1]
            for part in range(2):
                value = strip[part, :, order[0] * LANES : (order[0] + 1) * LANES]
                for block in order[1:]:
                    value = jnp.where(
                        lane_row + block * LANES >= start,
                        strip[part, :, block * LANES : (block + 1) * LANES],
                        value,
                    )
                cut[item, part, :, half * LANES : (half + 1) * LANES] = value


def wave_kernel(row_ref, live_ref, win, probe, intensity, table, grad):
    rows, window = win.shape[3:]
    row = row_ref[0]
    from_high = lax.broadcasted_iota(jnp.int32, (rows, window), 0) < row

    def object_part(section, part):
        outer = jnp.where(from_high, win[section, 2, part], win[section, 0, part])
        return jnp.concatenate([outer, win[section, 1, part]], axis=0)

    def give_back(section, real_part, imag_part):
        for part, value in ((0, real_part), (1, imag_part)):
            outer = value[:rows]
            grad[section, 0, part] = jnp.where(from_high, 0.0, outer)
            grad[section, 1, part] = value[rows:]
            grad[section, 2, part] = jnp.where(from_high, outer, 0.0)

    probe_re, probe_im = probe[0], probe[1]
    obj_re, obj_im = object_part(0, 0), object_part(0, 1)
    wave_re, wave_im = sandwich(
        probe_re * obj_re - probe_im * obj_im, probe_re * obj_im + probe_im * obj_re, table, 2, 3
    )
    obj_re, obj_im = object_part(1, 0), object_part(1, 1)
    far_re, far_im = sandwich(
        wave_re * obj_re - wave_im * obj_im, wave_re * obj_im + wave_im * obj_re, table, 0, 1
    )
    residual = live_ref[0] * (far_re * far_re + far_im * far_im - intensity[...])
    back_re, back_im = sandwich(residual * far_re, residual * far_im, table, 1, 0)
    give_back(1, wave_re * back_re + wave_im * back_im, wave_re * back_im - wave_im * back_re)
    back_re, back_im = sandwich(
        obj_re * back_re + obj_im * back_im, obj_re * back_im - obj_im * back_re, table, 3, 2
    )
    give_back(0, probe_re * back_re + probe_im * back_im, probe_re * back_im - probe_im * back_re)


def sum_kernel(starts, back, summed):
    rows, window = back.shape[2:]
    blocks = summed.shape[2] // LANES
    lane_row = lax.broadcasted_iota(jnp.int32, (1, LANES), 1)
    for block in range(blocks):
        half = slice((block % 2) * LANES, (block % 2 + 1) * LANES)
        for part in range(2):
            total = jnp.zeros((rows, LANES), jnp.float32)
            for item in range(6):
                offset = lane_row + block * LANES - jnp.full((1, LANES), starts[item], jnp.int32)
                inside = jnp.logical_and(offset >= 0, offset < window)
                total += jnp.where(inside, back[item, part, :, half], 0.0)
            summed[part, :, block * LANES : (block + 1) * LANES] = total


def solution(mesh):
    tiles = mesh.shape["tile"]
    up = [(t, t + 1) for t in range(tiles - 1)]
    down = [(t + 1, t) for t in range(tiles - 1)]
    swap = [(0, 1), (1, 0)]

    def crossed(pairs):
        return [(c * tiles + a, (1 - c) * tiles + b) for c in range(2) for a, b in pairs]

    def call(body, shape, scalars, arrays):
        return pl.pallas_call(
            body,
            out_shape=jax.ShapeDtypeStruct(shape, jnp.float32),
            in_specs=[
                pl.BlockSpec(memory_space=pltpu.SMEM if scalar else pltpu.VMEM)
                for scalar in scalars
            ],
            out_specs=pl.BlockSpec(memory_space=pltpu.VMEM),
            compiler_params=pltpu.CompilerParams(vmem_limit_bytes=40 * 1024 * 1024),
        )(*arrays)

    def exchange(low, own, high):
        core = lax.axis_index("cuts")

        def pick(pieces, same):
            first = (core == 0) == same
            return jnp.where(first, pieces[0], pieces[1])

        both = ("cuts", "tile")
        same = [
            lax.ppermute(pick(high, True), "tile", up),
            pick(own, True),
            lax.ppermute(pick(low, True), "tile", down),
        ]
        other = [
            lax.ppermute(pick(high, False), both, crossed(up)),
            lax.ppermute(pick(own, False), "cuts", swap),
            lax.ppermute(pick(low, False), both, crossed(down)),
        ]
        from_zero = [jnp.where(core == 0, s, o) for s, o in zip(same, other)]
        from_one = [jnp.where(core == 0, o, s) for s, o in zip(same, other)]
        return from_zero, from_one

    def local(object_slices, probe, positions, counts, intensity):
        window = probe.shape[-1]
        rows, ncolumns = object_slices.shape[2:]
        table = jnp.asarray(build_tables(window))
        core = lax.axis_index("cuts")
        below = lax.ppermute(positions, "tile", up)
        above = lax.ppermute(positions, "tile", down)
        starts = jnp.concatenate([below[:, 1], positions[:, 1], above[:, 1]])
        cut = call(
            cut_kernel, (6, 2, rows, window), (False, True), (object_slices[0], starts)
        )
        zero, one = exchange((cut[0], cut[1]), (cut[2], cut[3]), (cut[4], cut[5]))
        win = jnp.stack([jnp.stack(zero), jnp.stack(one)])
        rolled = call(
            functools.partial(roll_kernel, rows), probe.shape, (True, False), (positions, probe)
        )
        row = lax.dynamic_slice(positions[:, 0], (core,), (1,))
        row = row - (lax.axis_index("tile") - 1) * rows
        live = (core < counts).astype(jnp.float32)
        shot = lax.dynamic_index_in_dim(intensity, core, 0, keepdims=False)
        grad = call(
            wave_kernel,
            (2, 3, 2, rows, window),
            (True, True, False, False, False, False),
            (row, live, win, rolled, shot, table),
        )
        zero, one = exchange(
            (grad[0, 0], grad[1, 0]), (grad[0, 1], grad[1, 1]), (grad[0, 2], grad[1, 2])
        )
        back = jnp.stack([zero[0], one[0], zero[1], one[1], zero[2], one[2]])
        return call(sum_kernel, (2, rows, ncolumns), (True, False), (starts, back))[None]

    in_specs = (
        P("cuts", None, "tile", None),
        P(),
        P("tile", None),
        P("tile"),
        P("tile", None, None),
    )
    out_specs = P("cuts", None, "tile", None)
    return jax.shard_map(local, mesh=mesh, in_specs=in_specs, out_specs=out_specs, check_vma=False)
```

profile of v0, /device:TPU:25, one launch (start us, length us, event | category | flops | bytes accessed | tf_op | source)
XLA Modules:
  0.0 82.6 jit_solution(17120912054344478399)
XLA Ops:
  0.0 4.1 %collective-permute-start.1 = (s32[2,2]{1,0:T(2,128)}, s32[2,2]{1,0:T(2,128)S(1)}, u32[]{:S(2)}, u32[]{:S(2)}) collective-permute-start(s32[2,2]{1,0:T(2,128)} %pos.1), channel_id=1, source_target_pairs={{1,0},{2,1},{3,2},{4,3},{5,4},{6,5},{7,6},{8,7},{9,8},{10,9},{11,1... | collective-permute-start | bytes 56 | tf_op jit(solution)/shard_map/ppermute | solution.py:184
  4.1 1.9 %collective-permute-start = (s32[2,2]{1,0:T(2,128)}, s32[2,2]{1,0:T(2,128)S(1)}, u32[]{:S(2)}, u32[]{:S(2)}) collective-permute-start(s32[2,2]{1,0:T(2,128)} %pos.1), channel_id=1, source_target_pairs={{0,1},{1,2},{2,3},{3,4},{4,5},{5,6},{6,7},{7,8},{8,9},{9,10},{10,1... | collective-permute-start | bytes 56 | tf_op jit(solution)/shard_map/ppermute | solution.py:183
  7.1 3.3 %collective-permute-done = s32[2,2]{1,0:T(2,128)S(1)} collective-permute-done((s32[2,2]{1,0:T(2,128)}, s32[2,2]{1,0:T(2,128)S(1)}, u32[]{:S(2)}, u32[]{:S(2)}) %collective-permute-start) | collective-permute-done | bytes 48 | tf_op jit(solution)/shard_map/ppermute | solution.py:183
  10.7 1.6 %copy-done.2 = f32[1,2,128,2048]{3,2,1,0:T(8,128)S(1)} copy-done((f32[1,2,128,2048]{3,2,1,0:T(8,128)S(1)}, f32[1,2,128,2048]{3,2,1,0:T(8,128)}, u32[]{:S(2)}) %copy-start.2) | copy-done | bytes 2097176
  12.3 1.3 %shard_map.64 = f32[6,2,128,256]{3,2,1,0:T(8,128)S(1)} custom-call(f32[2,128,2048]{2,1,0:T(8,128)S(1)} %bitcast.69, s32[6]{0:T(128)S(1)} %pad_add_fusion.starts), custom_call_target="tpu_custom_call" | custom-call | tf_op jit(solution)/shard_map/pallas_call | solution.py:145
  13.6 1.1 %select_bitcast_fusion.13 = (f32[2,128,256]{2,1,0:T(8,128)}, f32[2,128,256]{2,1,0:T(8,128)}, f32[2,128,256]{2,1,0:T(8,128)}, f32[2,128,256]{2,1,0:T(8,128)}, f32[2,128,256]{2,1,0:T(8,128)}) fusion(f32[6,2,128,256]{3,2,1,0:T(8,128)S(1)} %shard_map.64, pred[]{:T(512)S(6)} %eq.4, pred[]{:T(512)S(6)} %eq.5), kind=kLoop, calls=%fused_computation.29 | loop fusion | flops 327680 | bytes 2883586 | tf_op jit(solution)/shard_map/jit(_where)/select_n | solution.py:161
  14.7 2.1 %collective-permute-start.4 = (f32[2,128,256]{2,1,0:T(8,128)}, f32[2,128,256]{2,1,0:T(8,128)}, u32[]{:S(2)}, u32[]{:S(2)}) collective-permute-start(f32[2,128,256]{2,1,0:T(8,128)} %get-tuple-element.15), channel_id=1, source_target_pairs={{0,16},{16,0},{1,17},{17,1},{2,18},{18,2},{3,19},{19,3},{4,20},{20... | collective-permute-start | bytes 786440 | tf_op jit(solution)/shard_map/ppermute | solution.py:171
  16.8 1.9 %collective-permute-start.5 = (f32[2,128,256]{2,1,0:T(8,128)}, f32[2,128,256]{2,1,0:T(8,128)}, u32[]{:S(2)}, u32[]{:S(2)}) collective-permute-start(f32[2,128,256]{2,1,0:T(8,128)} %get-tuple-element.13), channel_id=1, source_target_pairs={{1,0},{2,1},{3,2},{4,3},{5,4},{6,5},{7,6},{8,7},{9,8},{10,9},{11,1... | collective-permute-start | bytes 786440 | tf_op jit(solution)/shard_map/ppermute | solution.py:167
  18.7 2.6 %collective-permute-start.6 = (f32[2,128,256]{2,1,0:T(8,128)}, f32[2,128,256]{2,1,0:T(8,128)}, u32[]{:S(2)}, u32[]{:S(2)}) collective-permute-start(f32[2,128,256]{2,1,0:T(8,128)} %get-tuple-element.14), channel_id=1, source_target_pairs={{1,16},{2,17},{3,18},{4,19},{5,20},{6,21},{7,22},{8,23},{9,24},{10... | collective-permute-start | bytes 786440 | tf_op jit(solution)/shard_map/ppermute | solution.py:172
  24.0 2.7 %collective-permute-start.2 = (f32[2,128,256]{2,1,0:T(8,128)}, f32[2,128,256]{2,1,0:T(8,128)S(1)}, u32[]{:S(2)}, u32[]{:S(2)}) collective-permute-start(f32[2,128,256]{2,1,0:T(8,128)} %get-tuple-element.12), channel_id=1, source_target_pairs={{0,1},{1,2},{2,3},{3,4},{4,5},{5,6},{6,7},{7,8},{8,9},{9,10},{10,1... | collective-permute-start | bytes 786440 | tf_op jit(solution)/shard_map/ppermute | solution.py:165
  26.7 4.8 %collective-permute-start.3 = (f32[2,128,256]{2,1,0:T(8,128)}, f32[2,128,256]{2,1,0:T(8,128)S(1)}, u32[]{:S(2)}, u32[]{:S(2)}) collective-permute-start(f32[2,128,256]{2,1,0:T(8,128)} %get-tuple-element.16), channel_id=1, source_target_pairs={{0,17},{1,18},{2,19},{3,20},{4,21},{5,22},{6,23},{7,24},{8,25},{9,... | collective-permute-start | bytes 786440 | tf_op jit(solution)/shard_map/ppermute | solution.py:170
  33.2 1.1 %select_bitcast_fusion.7 = (f32[1,2,128,256]{3,2,1,0:T(8,128)S(1)}, f32[1,2,128,256]{3,2,1,0:T(8,128)S(1)}) fusion(f32[2,128,256]{2,1,0:T(8,128)} %collective-permute-done.5, f32[2,128,256]{2,1,0:T(8,128)} %collective-permute-done.6, pred[]{:T(512)S(6)} %eq.4), kind=kLoop, calls=%fused_computation.23 | loop fusion | flops 131072 | bytes 1048577 | tf_op jit(solution)/shard_map/stack | solution.py:190
  34.3 1.3 %collective-permute-done.2 = f32[2,128,256]{2,1,0:T(8,128)S(1)} collective-permute-done((f32[2,128,256]{2,1,0:T(8,128)}, f32[2,128,256]{2,1,0:T(8,128)S(1)}, u32[]{:S(2)}, u32[]{:S(2)}) %collective-permute-start.2) | collective-permute-done | bytes 262176 | tf_op jit(solution)/shard_map/ppermute | solution.py:165
  35.6 6.0 %collective-permute-done.3 = f32[2,128,256]{2,1,0:T(8,128)S(1)} collective-permute-done((f32[2,128,256]{2,1,0:T(8,128)}, f32[2,128,256]{2,1,0:T(8,128)S(1)}, u32[]{:S(2)}, u32[]{:S(2)}) %collective-permute-start.3) | collective-permute-done | bytes 262176 | tf_op jit(solution)/shard_map/ppermute | solution.py:170
  42.0 1.9 %copy-done.1 = bf16[4,2,512,512]{3,2,1,0:T(8,128)(2,1)S(1)} copy-done((bf16[4,2,512,512]{3,2,1,0:T(8,128)(2,1)S(1)}, bf16[4,2,512,512]{3,2,1,0:T(8,128)(2,1)}, u32[]{:S(2)}) %copy-start.1) | copy-done | bytes 4194328
  43.9 6.3 %shard_map.66 = f32[2,3,2,128,256]{4,3,2,1,0:T(8,128)S(1)} custom-call(s32[1]{0:T(128)S(6)} %sub.11.row_ref, f32[1]{0:T(128)S(6)} %convert_element_type.3.live_ref, f32[2,3,2,128,256]{4,3,2,1,0:T(8,128)S(1)} %pad_maximum_fusion.win, f32[2,256,256]{2,1,0:T(8,128)S(1)} %shard_map.65.probe, f32[256,256]{1,0:T(8,128)S(1)} %dynamic-slice_bitcast_fusion.intensity, ...), custom_call_target="tpu_custom_call" | custom-call | tf_op jit(solution)/shard_map/pallas_call | solution.py:145
  50.4 3.4 %collective-permute-start.7 = (f32[2,128,256]{2,1,0:T(8,128)S(1)}, f32[2,128,256]{2,1,0:T(8,128)S(1)}, u32[]{:S(2)}, u32[]{:S(2)}) collective-permute-start(f32[2,128,256]{2,1,0:T(8,128)S(1)} %get-tuple-element.10), channel_id=1, source_target_pairs={{0,1},{1,2},{2,3},{3,4},{4,5},{5,6},{6,7},{7,8},{8,9},{9,10},{10,1... | collective-permute-start | bytes 786440 | tf_op jit(solution)/shard_map/ppermute | solution.py:165
  53.7 5.5 %collective-permute-start.8 = (f32[2,128,256]{2,1,0:T(8,128)S(1)}, f32[2,128,256]{2,1,0:T(8,128)S(1)}, u32[]{:S(2)}, u32[]{:S(2)}) collective-permute-start(f32[2,128,256]{2,1,0:T(8,128)S(1)} %get-tuple-element.11), channel_id=1, source_target_pairs={{0,17},{1,18},{2,19},{3,20},{4,21},{5,22},{6,23},{7,24},{8,25},{9,... | collective-permute-start | bytes 786440 | tf_op jit(solution)/shard_map/ppermute | solution.py:170
  59.2 1.9 %collective-permute-start.11 = (f32[2,128,256]{2,1,0:T(8,128)S(1)}, f32[2,128,256]{2,1,0:T(8,128)S(1)}, u32[]{:S(2)}, u32[]{:S(2)}) collective-permute-start(f32[2,128,256]{2,1,0:T(8,128)S(1)} %get-tuple-element.7), channel_id=1, source_target_pairs={{1,16},{2,17},{3,18},{4,19},{5,20},{6,21},{7,22},{8,23},{9,24},{10... | collective-permute-start | bytes 786440 | tf_op jit(solution)/shard_map/ppermute | solution.py:172
  61.1 2.6 %collective-permute-start.10 = (f32[2,128,256]{2,1,0:T(8,128)S(1)}, f32[2,128,256]{2,1,0:T(8,128)S(1)}, u32[]{:S(2)}, u32[]{:S(2)}) collective-permute-start(f32[2,128,256]{2,1,0:T(8,128)S(1)} %get-tuple-element.8), channel_id=1, source_target_pairs={{1,0},{2,1},{3,2},{4,3},{5,4},{6,5},{7,6},{8,7},{9,8},{10,9},{11,1... | collective-permute-start | bytes 786440 | tf_op jit(solution)/shard_map/ppermute | solution.py:167
  64.2 3.6 %collective-permute-done.8 = f32[2,128,256]{2,1,0:T(8,128)S(1)} collective-permute-done((f32[2,128,256]{2,1,0:T(8,128)S(1)}, f32[2,128,256]{2,1,0:T(8,128)S(1)}, u32[]{:S(2)}, u32[]{:S(2)}) %collective-permute-start.8) | collective-permute-done | bytes 262176 | tf_op jit(solution)/shard_map/ppermute | solution.py:170
  68.0 7.3 %collective-permute-done.11 = f32[2,128,256]{2,1,0:T(8,128)S(1)} collective-permute-done((f32[2,128,256]{2,1,0:T(8,128)S(1)}, f32[2,128,256]{2,1,0:T(8,128)S(1)}, u32[]{:S(2)}, u32[]{:S(2)}) %collective-permute-start.11) | collective-permute-done | bytes 262176 | tf_op jit(solution)/shard_map/ppermute | solution.py:172
  75.3 4.4 %collective-permute-done.10 = f32[2,128,256]{2,1,0:T(8,128)S(1)} collective-permute-done((f32[2,128,256]{2,1,0:T(8,128)S(1)}, f32[2,128,256]{2,1,0:T(8,128)S(1)}, u32[]{:S(2)}, u32[]{:S(2)}) %collective-permute-start.10) | collective-permute-done | bytes 262176 | tf_op jit(solution)/shard_map/ppermute | solution.py:167
  79.9 2.7 %shard_map.67 = f32[2,128,2048]{2,1,0:T(8,128)} custom-call(s32[6]{0:T(128)S(1)} %pad_add_fusion.starts, f32[6,2,128,256]{3,2,1,0:T(8,128)S(1)} %bitcast_dynamic-update-slice_fusion.back), custom_call_target="tpu_custom_call" | custom-call | tf_op jit(solution)/shard_map/pallas_call | solution.py:145
  (33 shorter events, 5.6 us)
Async XLA Ops:
  0.0 21.3 %copy-start = (f32[2,256,256]{2,1,0:T(8,128)S(1)}, f32[2,256,256]{2,1,0:T(8,128)}, u32[]{:S(2)}) copy-start(f32[2,256,256]{2,1,0:T(8,128)} %param.10) | copy-start | bytes 1572868
  0.0 6.9 %collective-permute-start.1 = (s32[2,2]{1,0:T(2,128)}, s32[2,2]{1,0:T(2,128)S(1)}, u32[]{:S(2)}, u32[]{:S(2)}) collective-permute-start(s32[2,2]{1,0:T(2,128)} %pos.1), channel_id=1, source_target_pairs={{1,0},{2,1},{3,2},{4,3},{5,4},{6,5},{7,6},{8,7},{9,8},{10,9},{11,1... | collective-permute-start | bytes 56 | tf_op jit(solution)/shard_map/ppermute | solution.py:184
  4.1 6.3 %collective-permute-start = (s32[2,2]{1,0:T(2,128)}, s32[2,2]{1,0:T(2,128)S(1)}, u32[]{:S(2)}, u32[]{:S(2)}) collective-permute-start(s32[2,2]{1,0:T(2,128)} %pos.1), channel_id=1, source_target_pairs={{0,1},{1,2},{2,3},{3,4},{4,5},{5,6},{6,7},{7,8},{8,9},{9,10},{10,1... | collective-permute-start | bytes 56 | tf_op jit(solution)/shard_map/ppermute | solution.py:183
  10.7 1.6 %copy-start.2 = (f32[1,2,128,2048]{3,2,1,0:T(8,128)S(1)}, f32[1,2,128,2048]{3,2,1,0:T(8,128)}, u32[]{:S(2)}) copy-start(f32[1,2,128,2048]{3,2,1,0:T(8,128)} %param.6) | copy-start | bytes 6291460
  13.6 9.0 %copy-start.3 = (f32[2,256,256]{2,1,0:T(8,128)S(1)}, f32[2,256,256]{2,1,0:T(8,128)}, u32[]{:S(2)}) copy-start(f32[2,256,256]{2,1,0:T(8,128)} %probe.1) | copy-start | bytes 1572868
  13.6 8.9 %copy-start.4 = (s32[2,2]{1,0:T(2,128)S(1)}, s32[2,2]{1,0:T(2,128)}, u32[]{:S(2)}) copy-start(s32[2,2]{1,0:T(2,128)} %pos.1) | copy-start | bytes 52
  14.7 16.8 %collective-permute-start.4 = (f32[2,128,256]{2,1,0:T(8,128)}, f32[2,128,256]{2,1,0:T(8,128)}, u32[]{:S(2)}, u32[]{:S(2)}) collective-permute-start(f32[2,128,256]{2,1,0:T(8,128)} %get-tuple-element.15), channel_id=1, source_target_pairs={{0,16},{16,0},{1,17},{17,1},{2,18},{18,2},{3,19},{19,3},{4,20},{20... | collective-permute-start | bytes 786440 | tf_op jit(solution)/shard_map/ppermute | solution.py:171
  16.8 15.7 %collective-permute-start.5 = (f32[2,128,256]{2,1,0:T(8,128)}, f32[2,128,256]{2,1,0:T(8,128)}, u32[]{:S(2)}, u32[]{:S(2)}) collective-permute-start(f32[2,128,256]{2,1,0:T(8,128)} %get-tuple-element.13), channel_id=1, source_target_pairs={{1,0},{2,1},{3,2},{4,3},{5,4},{6,5},{7,6},{8,7},{9,8},{10,9},{11,1... | collective-permute-start | bytes 786440 | tf_op jit(solution)/shard_map/ppermute | solution.py:167
  18.7 14.5 %collective-permute-start.6 = (f32[2,128,256]{2,1,0:T(8,128)}, f32[2,128,256]{2,1,0:T(8,128)}, u32[]{:S(2)}, u32[]{:S(2)}) collective-permute-start(f32[2,128,256]{2,1,0:T(8,128)} %get-tuple-element.14), channel_id=1, source_target_pairs={{1,16},{2,17},{3,18},{4,19},{5,20},{6,21},{7,22},{8,23},{9,24},{10... | collective-permute-start | bytes 786440 | tf_op jit(solution)/shard_map/ppermute | solution.py:172
  24.0 11.6 %collective-permute-start.2 = (f32[2,128,256]{2,1,0:T(8,128)}, f32[2,128,256]{2,1,0:T(8,128)S(1)}, u32[]{:S(2)}, u32[]{:S(2)}) collective-permute-start(f32[2,128,256]{2,1,0:T(8,128)} %get-tuple-element.12), channel_id=1, source_target_pairs={{0,1},{1,2},{2,3},{3,4},{4,5},{5,6},{6,7},{7,8},{8,9},{9,10},{10,1... | collective-permute-start | bytes 786440 | tf_op jit(solution)/shard_map/ppermute | solution.py:165
  26.7 14.9 %collective-permute-start.3 = (f32[2,128,256]{2,1,0:T(8,128)}, f32[2,128,256]{2,1,0:T(8,128)S(1)}, u32[]{:S(2)}, u32[]{:S(2)}) collective-permute-start(f32[2,128,256]{2,1,0:T(8,128)} %get-tuple-element.16), channel_id=1, source_target_pairs={{0,17},{1,18},{2,19},{3,20},{4,21},{5,22},{6,23},{7,24},{8,25},{9,... | collective-permute-start | bytes 786440 | tf_op jit(solution)/shard_map/ppermute | solution.py:170
  41.7 2.2 %copy-start.1 = (bf16[4,2,512,512]{3,2,1,0:T(8,128)(2,1)S(1)}, bf16[4,2,512,512]{3,2,1,0:T(8,128)(2,1)}, u32[]{:S(2)}) copy-start(bf16[4,2,512,512]{3,2,1,0:T(8,128)(2,1)} %constant.27.clone.table) | copy-start | bytes 12582916
  50.4 13.8 %collective-permute-start.7 = (f32[2,128,256]{2,1,0:T(8,128)S(1)}, f32[2,128,256]{2,1,0:T(8,128)S(1)}, u32[]{:S(2)}, u32[]{:S(2)}) collective-permute-start(f32[2,128,256]{2,1,0:T(8,128)S(1)} %get-tuple-element.10), channel_id=1, source_target_pairs={{0,1},{1,2},{2,3},{3,4},{4,5},{5,6},{6,7},{7,8},{8,9},{9,10},{10,1... | collective-permute-start | bytes 786440 | tf_op jit(solution)/shard_map/ppermute | solution.py:165
  53.7 14.1 %collective-permute-start.8 = (f32[2,128,256]{2,1,0:T(8,128)S(1)}, f32[2,128,256]{2,1,0:T(8,128)S(1)}, u32[]{:S(2)}, u32[]{:S(2)}) collective-permute-start(f32[2,128,256]{2,1,0:T(8,128)S(1)} %get-tuple-element.11), channel_id=1, source_target_pairs={{0,17},{1,18},{2,19},{3,20},{4,21},{5,22},{6,23},{7,24},{8,25},{9,... | collective-permute-start | bytes 786440 | tf_op jit(solution)/shard_map/ppermute | solution.py:170
  59.2 16.1 %collective-permute-start.11 = (f32[2,128,256]{2,1,0:T(8,128)S(1)}, f32[2,128,256]{2,1,0:T(8,128)S(1)}, u32[]{:S(2)}, u32[]{:S(2)}) collective-permute-start(f32[2,128,256]{2,1,0:T(8,128)S(1)} %get-tuple-element.7), channel_id=1, source_target_pairs={{1,16},{2,17},{3,18},{4,19},{5,20},{6,21},{7,22},{8,23},{9,24},{10... | collective-permute-start | bytes 786440 | tf_op jit(solution)/shard_map/ppermute | solution.py:172
  61.1 18.6 %collective-permute-start.10 = (f32[2,128,256]{2,1,0:T(8,128)S(1)}, f32[2,128,256]{2,1,0:T(8,128)S(1)}, u32[]{:S(2)}, u32[]{:S(2)}) collective-permute-start(f32[2,128,256]{2,1,0:T(8,128)S(1)} %get-tuple-element.8), channel_id=1, source_target_pairs={{1,0},{2,1},{3,2},{4,3},{5,4},{6,5},{7,6},{8,7},{9,8},{10,9},{11,1... | collective-permute-start | bytes 786440 | tf_op jit(solution)/shard_map/ppermute | solution.py:167
  63.7 4.2 %collective-permute-start.9 = (f32[2,128,256]{2,1,0:T(8,128)S(1)}, f32[2,128,256]{2,1,0:T(8,128)S(1)}, u32[]{:S(2)}, u32[]{:S(2)}) collective-permute-start(f32[2,128,256]{2,1,0:T(8,128)S(1)} %get-tuple-element.9), channel_id=1, source_target_pairs={{0,16},{16,0},{1,17},{17,1},{2,18},{18,2},{3,19},{19,3},{4,20},{20... | collective-permute-start | bytes 786440 | tf_op jit(solution)/shard_map/ppermute | solution.py:171
where the time goes:
time: 83.9 us; the launch traced here: 82.6 us
  starting transfers between devices  33.9 us (40%)
  waiting for transfers between devices  26.7 us (32%)
  Pallas kernels  11.1 us (13%)
  local copies, waits for them, and re-layouts  5.32 us (6%)
  other arithmetic  4 us (5%)
  between operations  1.54 us (2%)
    pallas_call x4, Pallas kernels, call(): pl.pallas_call(body, out_shape=jax.ShapeDtypeStruct(shape, jnp.float32),...  11.1 us
    ppermute x2, starting transfers between devices, exchange(): lax.ppermute(pick(high, False), both, crossed(up))  10.3 us
    ppermute x2, waiting for transfers between devices, exchange(): lax.ppermute(pick(high, False), both, crossed(up))  9.67 us
    ppermute x2, waiting for transfers between devices, exchange(): lax.ppermute(pick(low, False), both, crossed(down))  7.98 us
    ppermute x2, starting transfers between devices, exchange(): lax.ppermute(pick(high, True), 'tile', up)  6.06 us
    ppermute x2, starting transfers between devices, exchange(): lax.ppermute(pick(low, False), both, crossed(down))  4.5 us
    ppermute x2, starting transfers between devices, exchange(): lax.ppermute(pick(low, True), 'tile', down)  4.47 us
    ppermute x2, waiting for transfers between devices, exchange(): lax.ppermute(pick(low, True), 'tile', down)  4.45 us
  transfers between devices with their start and end apart: 12, of which 7 were waited for; matrix products, arithmetic and copies ran while one was open for 5% of the time, Pallas kernels for 1%

commit v1 on v0

--- a/solution.py
+++ b/solution.py
@@ -65,7 +65,7 @@
         rolled[part] = pltpu.roll(pltpu.roll(probe[part], row, 0), turn, 1)
 
 
-def cut_kernel(strip, starts, cut):
+def cut_kernel(strip, starts, *cut):
     blocks = strip.shape[2] // LANES
     lane_row = lax.broadcasted_iota(jnp.int32, (1, LANES), 1)
     for item in range(6):
@@ -80,24 +80,32 @@
                         strip[part, :, block * LANES : (block + 1) * LANES],
                         value,
                     )
-                cut[item, part, :, half * LANES : (half + 1) * LANES] = value
-
-
-def wave_kernel(row_ref, live_ref, win, probe, intensity, table, grad):
-    rows, window = win.shape[3:]
+                cut[item][part, :, half * LANES : (half + 1) * LANES] = value
+
+
+def wave_kernel(row_ref, live_ref, probe, intensity, table, *pieces):
+    win, grad = pieces[:6], pieces[6:]
+    rows, window = win[0].shape[1:]
+    core = lax.axis_index("cuts")
     row = row_ref[0]
     from_high = lax.broadcasted_iota(jnp.int32, (rows, window), 0) < row
 
     def object_part(section, part):
-        outer = jnp.where(from_high, win[section, 2, part], win[section, 0, part])
-        return jnp.concatenate([outer, win[section, 1, part]], axis=0)
+        low, own, high = (
+            jnp.where(core == section, win[2 * place][part], win[2 * place + 1][part])
+            for place in range(3)
+        )
+        return jnp.concatenate([jnp.where(from_high, high, low), own], axis=0)
 
     def give_back(section, real_part, imag_part):
         for part, value in ((0, real_part), (1, imag_part)):
             outer = value[:rows]
-            grad[section, 0, part] = jnp.where(from_high, 0.0, outer)
-            grad[section, 1, part] = value[rows:]
-            grad[section, 2, part] = jnp.where(from_high, outer, 0.0)
+            parts = (jnp.where(from_high, 0.0, outer), value[rows:], jnp.where(from_high, outer, 0.0))
+            for far in range(2):
+                @pl.when(core == abs(section - far))
+                def _():
+                    for place in range(3):
+                        grad[2 * place + far][part] = parts[place]
 
     probe_re, probe_im = probe[0], probe[1]
     obj_re, obj_im = object_part(0, 0), object_part(0, 1)
@@ -117,8 +125,9 @@
     give_back(0, probe_re * back_re + probe_im * back_im, probe_re * back_im - probe_im * back_re)
 
 
-def sum_kernel(starts, back, summed):
-    rows, window = back.shape[2:]
+def sum_kernel(starts, *pieces):
+    back, summed = pieces[:6], pieces[6]
+    rows, window = back[0].shape[1:]
     blocks = summed.shape[2] // LANES
     lane_row = lax.broadcasted_iota(jnp.int32, (1, LANES), 1)
     for block in range(blocks):
@@ -128,7 +137,7 @@
             for item in range(6):
                 offset = lane_row + block * LANES - jnp.full((1, LANES), starts[item], jnp.int32)
                 inside = jnp.logical_and(offset >= 0, offset < window)
-                total += jnp.where(inside, back[item, part, :, half], 0.0)
+                total += jnp.where(inside, back[item][part, :, half], 0.0)
             summed[part, :, block * LANES : (block + 1) * LANES] = total
 
 
@@ -141,39 +150,29 @@
     def crossed(pairs):
         return [(c * tiles + a, (1 - c) * tiles + b) for c in range(2) for a, b in pairs]
 
-    def call(body, shape, scalars, arrays):
+    def call(body, shapes, scalars, arrays):
         return pl.pallas_call(
             body,
-            out_shape=jax.ShapeDtypeStruct(shape, jnp.float32),
+            out_shape=[jax.ShapeDtypeStruct(shape, jnp.float32) for shape in shapes],
             in_specs=[
-                pl.BlockSpec(memory_space=pltpu.SMEM if scalar else pltpu.VMEM)
-                for scalar in scalars
+                pl.BlockSpec(memory_space=pltpu.SMEM if index in scalars else pltpu.VMEM)
+                for index in range(len(arrays))
             ],
-            out_specs=pl.BlockSpec(memory_space=pltpu.VMEM),
+            out_specs=[pl.BlockSpec(memory_space=pltpu.VMEM)] * len(shapes),
             compiler_params=pltpu.CompilerParams(vmem_limit_bytes=40 * 1024 * 1024),
         )(*arrays)
 
-    def exchange(low, own, high):
-        core = lax.axis_index("cuts")
-
-        def pick(pieces, same):
-            first = (core == 0) == same
-            return jnp.where(first, pieces[0], pieces[1])
-
+    def exchange(pieces):
+        low_same, low_other, own_same, own_other, high_same, high_other = pieces
         both = ("cuts", "tile")
-        same = [
-            lax.ppermute(pick(high, True), "tile", up),
-            pick(own, True),
-            lax.ppermute(pick(low, True), "tile", down),
-        ]
-        other = [
-            lax.ppermute(pick(high, False), both, crossed(up)),
-            lax.ppermute(pick(own, False), "cuts", swap),
-            lax.ppermute(pick(low, False), both, crossed(down)),
-        ]
-        from_zero = [jnp.where(core == 0, s, o) for s, o in zip(same, other)]
-        from_one = [jnp.where(core == 0, o, s) for s, o in zip(same, other)]
-        return from_zero, from_one
+        return (
+            lax.ppermute(high_same, "tile", up),
+            lax.ppermute(high_other, both, crossed(up)),
+            own_same,
+            lax.ppermute(own_other, "cuts", swap),
+            lax.ppermute(low_same, "tile", down),
+            lax.ppermute(low_other, both, crossed(down)),
+        )
 
     def local(object_slices, probe, positions, counts, intensity):
         window = probe.shape[-1]
@@ -182,30 +181,21 @@
         core = lax.axis_index("cuts")
         below = lax.ppermute(positions, "tile", up)
         above = lax.ppermute(positions, "tile", down)
-        starts = jnp.concatenate([below[:, 1], positions[:, 1], above[:, 1]])
-        cut = call(
-            cut_kernel, (6, 2, rows, window), (False, True), (object_slices[0], starts)
-        )
-        zero, one = exchange((cut[0], cut[1]), (cut[2], cut[3]), (cut[4], cut[5]))
-        win = jnp.stack([jnp.stack(zero), jnp.stack(one)])
-        rolled = call(
-            functools.partial(roll_kernel, rows), probe.shape, (True, False), (positions, probe)
+        around = jnp.stack([below[:, 1], positions[:, 1], above[:, 1]])
+        starts = jnp.where(core == 0, around, around[:, ::-1]).reshape(-1)
+        piece = (2, rows, window)
+        cut = call(cut_kernel, [piece] * 6, (1,), (object_slices[0], starts))
+        win = exchange(cut)
+        (rolled,) = call(
+            functools.partial(roll_kernel, rows), [probe.shape], (0,), (positions, probe)
         )
         row = lax.dynamic_slice(positions[:, 0], (core,), (1,))
         row = row - (lax.axis_index("tile") - 1) * rows
         live = (core < counts).astype(jnp.float32)
         shot = lax.dynamic_index_in_dim(intensity, core, 0, keepdims=False)
-        grad = call(
-            wave_kernel,
-            (2, 3, 2, rows, window),
-            (True, True, False, False, False, False),
-            (row, live, win, rolled, shot, table),
-        )
-        zero, one = exchange(
-            (grad[0, 0], grad[1, 0]), (grad[0, 1], grad[1, 1]), (grad[0, 2], grad[1, 2])
-        )
-        back = jnp.stack([zero[0], one[0], zero[1], one[1], zero[2], one[2]])
-        return call(sum_kernel, (2, rows, ncolumns), (True, False), (starts, back))[None]
+        grad = call(wave_kernel, [piece] * 6, (0, 1), (row, live, rolled, shot, table) + win)
+        back = exchange(grad)
+        return call(sum_kernel, [(2, rows, ncolumns)], (0,), (starts,) + back)[0][None]
 
     in_specs = (
         P("cuts", None, "tile", None),

time: 83.9 us -> 82.2 us (0.980); the launches traced: 82.6 us -> 81.7 us
  other arithmetic: 4 us -> 0.02 us
  waiting for transfers between devices: 26.7 us -> 27.9 us
  Pallas kernels: 11.1 us -> 12.1 us
    another operation x6 -> x1, other arithmetic: 2.46 us -> 0.01 us  [local(): around = jnp.stack([below[:, 1], positions[:, 1], above[:, 1]])]
    select_n x2 -> x1, other arithmetic: 1.26 us -> 0.01 us  [local(): starts = jnp.where(core == 0, around, around[:, ::-1]).reshape(-1)]
    ppermute x10, waiting for transfers between devices: 23.4 us -> 24.6 us  [the longest x2 13.1 us: exchange(): lax.ppermute(low_other, both, crossed(down))]
    pallas_call x4, Pallas kernels: 11.1 us -> 12.1 us  [call(): pl.pallas_call(body, out_shape=[jax.ShapeDtypeStruct(shape, jnp.float32)...]
  transfers between devices with their start and end apart: 12 -> 12, of which waited for: 7 -> 6; matrix products, arithmetic and copies ran while one was open for 5% -> 2% of each run, Pallas kernels for 1% -> 1%
where the time goes in v1:
time: 82.2 us; the launch traced here: 81.7 us
  starting transfers between devices  34.3 us (42%)
  waiting for transfers between devices  27.9 us (34%)
  Pallas kernels  12.1 us (15%)
  local copies, waits for them, and re-layouts  5.85 us (7%)
  between operations  1.54 us (2%)
    ppermute x2, waiting for transfers between devices, exchange(): lax.ppermute(low_other, both, crossed(down))  13.1 us
    pallas_call x4, Pallas kernels, call(): pl.pallas_call(body, out_shape=[jax.ShapeDtypeStruct(shape, jnp.float32)...  12.1 us
    ppermute x2, starting transfers between devices, exchange(): lax.ppermute(high_other, both, crossed(up))  11.6 us
    ppermute x2, waiting for transfers between devices, exchange(): lax.ppermute(low_same, 'tile', down)  7.76 us
    ppermute x2, starting transfers between devices, exchange(): lax.ppermute(low_same, 'tile', down)  6.57 us
    ppermute x2, starting transfers between devices, exchange(): lax.ppermute(low_other, both, crossed(down))  6.21 us
    ppermute x1, starting transfers between devices, local(): above = lax.ppermute(positions, 'tile', down)  4.08 us
    ppermute x2, starting transfers between devices, exchange(): lax.ppermute(high_same, 'tile', up)  3.83 us
  transfers between devices with their start and end apart: 12, of which 6 were waited for; matrix products, arithmetic and copies ran while one was open for 2% of the time, Pallas kernels for 1%

profile of v1, /device:TPU:25, one launch (start us, length us, event | category | flops | bytes accessed | tf_op | source)
XLA Modules:
  0.0 81.7 jit_solution(18256001973788924116)
XLA Ops:
  0.0 4.1 %collective-permute-start.1 = (s32[2,2]{1,0:T(2,128)}, s32[2,2]{1,0:T(2,128)S(1)}, u32[]{:S(2)}, u32[]{:S(2)}) collective-permute-start(s32[2,2]{1,0:T(2,128)} %pos.1), channel_id=1, source_target_pairs={{1,0},{2,1},{3,2},{4,3},{5,4},{6,5},{7,6},{8,7},{9,8},{10,9},{11,1... | collective-permute-start | bytes 56 | tf_op jit(solution)/shard_map/ppermute | solution.py:183
  4.1 1.9 %collective-permute-start = (s32[2,2]{1,0:T(2,128)}, s32[2,2]{1,0:T(2,128)S(1)}, u32[]{:S(2)}, u32[]{:S(2)}) collective-permute-start(s32[2,2]{1,0:T(2,128)} %pos.1), channel_id=1, source_target_pairs={{0,1},{1,2},{2,3},{3,4},{4,5},{5,6},{6,7},{7,8},{8,9},{9,10},{10,1... | collective-permute-start | bytes 56 | tf_op jit(solution)/shard_map/ppermute | solution.py:182
  6.0 0.9 %fusion = (s32[2,1]{1,0:T(2,128)S(1)}, s32[2]{0:T(128)S(1)}) fusion(s32[2,2]{1,0:T(2,128)} %pos.1), kind=kLoop, calls=%fused_computation.7 | loop fusion | bytes 32 | tf_op jit(solution)/shard_map/slice | solution.py:192
  7.1 3.3 %collective-permute-done = s32[2,2]{1,0:T(2,128)S(1)} collective-permute-done((s32[2,2]{1,0:T(2,128)}, s32[2,2]{1,0:T(2,128)S(1)}, u32[]{:S(2)}, u32[]{:S(2)}) %collective-permute-start) | collective-permute-done | bytes 48 | tf_op jit(solution)/shard_map/ppermute | solution.py:182
  10.8 1.6 %copy-done.2 = f32[1,2,128,2048]{3,2,1,0:T(8,128)S(1)} copy-done((f32[1,2,128,2048]{3,2,1,0:T(8,128)S(1)}, f32[1,2,128,2048]{3,2,1,0:T(8,128)}, u32[]{:S(2)}) %copy-start.2) | copy-done | bytes 2097176
  12.4 2.2 %shard_map.65 = (f32[2,128,256]{2,1,0:T(8,128)}, f32[2,128,256]{2,1,0:T(8,128)S(1)}, f32[2,128,256]{2,1,0:T(8,128)S(1)}, f32[2,128,256]{2,1,0:T(8,128)}, f32[2,128,256]{2,1,0:T(8,128)}, /*index=5*/f32[2,128,256]{2,1,0:T(8,128)}) custom-call(f32[2,128,2048]{2,1,0:T(8,128)S(1)} %bitcast.10, s32[6]{0:T(128)S(1)} %reshape.4.starts), custom_call_target="tpu_custom_call" | custom-call | tf_op jit(solution)/shard_map/pallas_call | solution.py:154
  14.6 1.9 %collective-permute-start.2 = (f32[2,128,256]{2,1,0:T(8,128)}, f32[2,128,256]{2,1,0:T(8,128)S(1)}, u32[]{:S(2)}, u32[]{:S(2)}) collective-permute-start(f32[2,128,256]{2,1,0:T(8,128)} %get-tuple-element.17), channel_id=1, source_target_pairs={{0,1},{1,2},{2,3},{3,4},{4,5},{5,6},{6,7},{7,8},{8,9},{9,10},{10,1... | collective-permute-start | bytes 786440 | tf_op jit(solution)/shard_map/ppermute | solution.py:169
  16.5 4.8 %collective-permute-start.3 = (f32[2,128,256]{2,1,0:T(8,128)}, f32[2,128,256]{2,1,0:T(8,128)S(1)}, u32[]{:S(2)}, u32[]{:S(2)}) collective-permute-start(f32[2,128,256]{2,1,0:T(8,128)} %get-tuple-element.18), channel_id=1, source_target_pairs={{0,17},{1,18},{2,19},{3,20},{4,21},{5,22},{6,23},{7,24},{8,25},{9,... | collective-permute-start | bytes 786440 | tf_op jit(solution)/shard_map/ppermute | solution.py:170
  21.4 4.6 %collective-permute-start.5 = (f32[2,128,256]{2,1,0:T(8,128)}, f32[2,128,256]{2,1,0:T(8,128)S(1)}, u32[]{:S(2)}, u32[]{:S(2)}) collective-permute-start(f32[2,128,256]{2,1,0:T(8,128)} %get-tuple-element.21), channel_id=1, source_target_pairs={{1,0},{2,1},{3,2},{4,3},{5,4},{6,5},{7,6},{8,7},{9,8},{10,9},{11,1... | collective-permute-start | bytes 786440 | tf_op jit(solution)/shard_map/ppermute | solution.py:173
  26.0 3.9 %collective-permute-start.6 = (f32[2,128,256]{2,1,0:T(8,128)S(1)}, f32[2,128,256]{2,1,0:T(8,128)S(1)}, u32[]{:S(2)}, u32[]{:S(2)}) collective-permute-start(f32[2,128,256]{2,1,0:T(8,128)S(1)} %get-tuple-element.22), channel_id=1, source_target_pairs={{1,16},{2,17},{3,18},{4,19},{5,20},{6,21},{7,22},{8,23},{9,24},{10... | collective-permute-start | bytes 786440 | tf_op jit(solution)/shard_map/ppermute | solution.py:174
  30.6 0.8 shard_map.64.probe
  31.4 0.6 constant_dynamic-slice_fusion
  32.8 1.0 %collective-permute-done.5.pieces_4_ = f32[2,128,256]{2,1,0:T(8,128)S(1)} collective-permute-done((f32[2,128,256]{2,1,0:T(8,128)}, f32[2,128,256]{2,1,0:T(8,128)S(1)}, u32[]{:S(2)}, u32[]{:S(2)}) %collective-permute-start.5) | collective-permute-done | bytes 262176 | tf_op jit(solution)/shard_map/ppermute | solution.py:173
  33.7 7.0 %collective-permute-done.6.pieces_5_ = f32[2,128,256]{2,1,0:T(8,128)S(1)} collective-permute-done((f32[2,128,256]{2,1,0:T(8,128)S(1)}, f32[2,128,256]{2,1,0:T(8,128)S(1)}, u32[]{:S(2)}, u32[]{:S(2)}) %collective-permute-start.6) | collective-permute-done | bytes 262176 | tf_op jit(solution)/shard_map/ppermute | solution.py:174
  40.7 2.2 %copy-done.1 = bf16[4,2,512,512]{3,2,1,0:T(8,128)(2,1)S(1)} copy-done((bf16[4,2,512,512]{3,2,1,0:T(8,128)(2,1)S(1)}, bf16[4,2,512,512]{3,2,1,0:T(8,128)(2,1)}, u32[]{:S(2)}) %copy-start.1) | copy-done | bytes 4194328
  42.9 6.4 %shard_map.66 = (f32[2,128,256]{2,1,0:T(8,128)S(1)}, f32[2,128,256]{2,1,0:T(8,128)S(1)}, f32[2,128,256]{2,1,0:T(8,128)S(1)}, f32[2,128,256]{2,1,0:T(8,128)S(1)},...) custom-call(s32[1]{0:T(128)S(6)} %sub.11.row_ref, f32[1]{0:T(128)S(6)} %convert_element_type.3.live_ref, ...), custom_call_target="tpu_custom_call" | custom-call | tf_op jit(solution)/shard_map/pallas_call | solution.py:154
  49.4 1.9 %collective-permute-start.7 = (f32[2,128,256]{2,1,0:T(8,128)S(1)}, f32[2,128,256]{2,1,0:T(8,128)S(1)}, u32[]{:S(2)}, u32[]{:S(2)}) collective-permute-start(f32[2,128,256]{2,1,0:T(8,128)S(1)} %get-tuple-element.23), channel_id=1, source_target_pairs={{0,1},{1,2},{2,3},{3,4},{4,5},{5,6},{6,7},{7,8},{8,9},{9,10},{10,1... | collective-permute-start | bytes 786440 | tf_op jit(solution)/shard_map/ppermute | solution.py:169
  51.3 6.8 %collective-permute-start.8 = (f32[2,128,256]{2,1,0:T(8,128)S(1)}, f32[2,128,256]{2,1,0:T(8,128)S(1)}, u32[]{:S(2)}, u32[]{:S(2)}) collective-permute-start(f32[2,128,256]{2,1,0:T(8,128)S(1)} %get-tuple-element.24), channel_id=1, source_target_pairs={{0,17},{1,18},{2,19},{3,20},{4,21},{5,22},{6,23},{7,24},{8,25},{9,... | collective-permute-start | bytes 786440 | tf_op jit(solution)/shard_map/ppermute | solution.py:170
  58.2 1.9 %collective-permute-start.10 = (f32[2,128,256]{2,1,0:T(8,128)S(1)}, f32[2,128,256]{2,1,0:T(8,128)S(1)}, u32[]{:S(2)}, u32[]{:S(2)}) collective-permute-start(f32[2,128,256]{2,1,0:T(8,128)S(1)} %get-tuple-element.27), channel_id=1, source_target_pairs={{1,0},{2,1},{3,2},{4,3},{5,4},{6,5},{7,6},{8,7},{9,8},{10,9},{11,1... | collective-permute-start | bytes 786440 | tf_op jit(solution)/shard_map/ppermute | solution.py:173
  60.1 2.3 %collective-permute-start.11 = (f32[2,128,256]{2,1,0:T(8,128)S(1)}, f32[2,128,256]{2,1,0:T(8,128)S(1)}, u32[]{:S(2)}, u32[]{:S(2)}) collective-permute-start(f32[2,128,256]{2,1,0:T(8,128)S(1)} %get-tuple-element.28), channel_id=1, source_target_pairs={{1,16},{2,17},{3,18},{4,19},{5,20},{6,21},{7,22},{8,23},{9,24},{10... | collective-permute-start | bytes 786440 | tf_op jit(solution)/shard_map/ppermute | solution.py:174
  62.4 3.7 %collective-permute-done.8.pieces_1_ = f32[2,128,256]{2,1,0:T(8,128)S(1)} collective-permute-done((f32[2,128,256]{2,1,0:T(8,128)S(1)}, f32[2,128,256]{2,1,0:T(8,128)S(1)}, u32[]{:S(2)}, u32[]{:S(2)}) %collective-permute-start.8) | collective-permute-done | bytes 262176 | tf_op jit(solution)/shard_map/ppermute | solution.py:170
  66.1 6.8 %collective-permute-done.10.pieces_4_ = f32[2,128,256]{2,1,0:T(8,128)S(1)} collective-permute-done((f32[2,128,256]{2,1,0:T(8,128)S(1)}, f32[2,128,256]{2,1,0:T(8,128)S(1)}, u32[]{:S(2)}, u32[]{:S(2)}) %collective-permute-start.10) | collective-permute-done | bytes 262176 | tf_op jit(solution)/shard_map/ppermute | solution.py:173
  72.9 6.2 %collective-permute-done.11.pieces_5_ = f32[2,128,256]{2,1,0:T(8,128)S(1)} collective-permute-done((f32[2,128,256]{2,1,0:T(8,128)S(1)}, f32[2,128,256]{2,1,0:T(8,128)S(1)}, u32[]{:S(2)}, u32[]{:S(2)}) %collective-permute-start.11) | collective-permute-done | bytes 262176 | tf_op jit(solution)/shard_map/ppermute | solution.py:174
  79.0 2.7 %shard_map.67 = f32[2,128,2048]{2,1,0:T(8,128)} custom-call(s32[6]{0:T(128)S(1)} %reshape.4.starts, f32[2,128,256]{2,1,0:T(8,128)S(1)} %collective-permute-done.7.pieces_0_, f32[2,128,256]{2,1,0:T(8,128)S(1)} %collective-permute-done.8.pieces_1_, f32[2,128,256]{2,1,0:T(8,128)S(1)} %get-tuple-element.25.pieces_2_, ...), custom_call_target="tpu_custom_call" | custom-call | tf_op jit(solution)/shard_map/pallas_call | solution.py:154
  (23 shorter events, 0.8 us)
Async XLA Ops:
  0.0 32.7 %copy-start = (f32[2,256,256]{2,1,0:T(8,128)S(1)}, f32[2,256,256]{2,1,0:T(8,128)}, u32[]{:S(2)}) copy-start(f32[2,256,256]{2,1,0:T(8,128)} %param.10) | copy-start | bytes 1572868
  0.0 30.6 %copy-start.4 = (s32[2,2]{1,0:T(2,128)S(1)}, s32[2,2]{1,0:T(2,128)}, u32[]{:S(2)}) copy-start(s32[2,2]{1,0:T(2,128)} %pos.1) | copy-start | bytes 52
  0.0 6.9 %collective-permute-start.1 = (s32[2,2]{1,0:T(2,128)}, s32[2,2]{1,0:T(2,128)S(1)}, u32[]{:S(2)}, u32[]{:S(2)}) collective-permute-start(s32[2,2]{1,0:T(2,128)} %pos.1), channel_id=1, source_target_pairs={{1,0},{2,1},{3,2},{4,3},{5,4},{6,5},{7,6},{8,7},{9,8},{10,9},{11,1... | collective-permute-start | bytes 56 | tf_op jit(solution)/shard_map/ppermute | solution.py:183
  4.1 6.3 %collective-permute-start = (s32[2,2]{1,0:T(2,128)}, s32[2,2]{1,0:T(2,128)S(1)}, u32[]{:S(2)}, u32[]{:S(2)}) collective-permute-start(s32[2,2]{1,0:T(2,128)} %pos.1), channel_id=1, source_target_pairs={{0,1},{1,2},{2,3},{3,4},{4,5},{5,6},{6,7},{7,8},{8,9},{9,10},{10,1... | collective-permute-start | bytes 56 | tf_op jit(solution)/shard_map/ppermute | solution.py:182
  10.8 1.6 %copy-start.2 = (f32[1,2,128,2048]{3,2,1,0:T(8,128)S(1)}, f32[1,2,128,2048]{3,2,1,0:T(8,128)}, u32[]{:S(2)}) copy-start(f32[1,2,128,2048]{3,2,1,0:T(8,128)} %param.6) | copy-start | bytes 6291460
  12.4 18.2 %copy-start.3 = (f32[2,256,256]{2,1,0:T(8,128)S(1)}, f32[2,256,256]{2,1,0:T(8,128)}, u32[]{:S(2)}) copy-start(f32[2,256,256]{2,1,0:T(8,128)} %probe.1) | copy-start | bytes 1572868
  14.6 18.2 %collective-permute-start.2 = (f32[2,128,256]{2,1,0:T(8,128)}, f32[2,128,256]{2,1,0:T(8,128)S(1)}, u32[]{:S(2)}, u32[]{:S(2)}) collective-permute-start(f32[2,128,256]{2,1,0:T(8,128)} %get-tuple-element.17), channel_id=1, source_target_pairs={{0,1},{1,2},{2,3},{3,4},{4,5},{5,6},{6,7},{7,8},{8,9},{9,10},{10,1... | collective-permute-start | bytes 786440 | tf_op jit(solution)/shard_map/ppermute | solution.py:169
  16.5 16.3 %collective-permute-start.3 = (f32[2,128,256]{2,1,0:T(8,128)}, f32[2,128,256]{2,1,0:T(8,128)S(1)}, u32[]{:S(2)}, u32[]{:S(2)}) collective-permute-start(f32[2,128,256]{2,1,0:T(8,128)} %get-tuple-element.18), channel_id=1, source_target_pairs={{0,17},{1,18},{2,19},{3,20},{4,21},{5,22},{6,23},{7,24},{8,25},{9,... | collective-permute-start | bytes 786440 | tf_op jit(solution)/shard_map/ppermute | solution.py:170
  21.3 11.5 %collective-permute-start.4 = (f32[2,128,256]{2,1,0:T(8,128)}, f32[2,128,256]{2,1,0:T(8,128)S(1)}, u32[]{:S(2)}, u32[]{:S(2)}) collective-permute-start(f32[2,128,256]{2,1,0:T(8,128)} %get-tuple-element.20), channel_id=1, source_target_pairs={{0,16},{16,0},{1,17},{17,1},{2,18},{18,2},{3,19},{19,3},{4,20},{20... | collective-permute-start | bytes 786440 | tf_op jit(solution)/shard_map/ppermute | solution.py:172
  21.4 12.4 %collective-permute-start.5 = (f32[2,128,256]{2,1,0:T(8,128)}, f32[2,128,256]{2,1,0:T(8,128)S(1)}, u32[]{:S(2)}, u32[]{:S(2)}) collective-permute-start(f32[2,128,256]{2,1,0:T(8,128)} %get-tuple-element.21), channel_id=1, source_target_pairs={{1,0},{2,1},{3,2},{4,3},{5,4},{6,5},{7,6},{8,7},{9,8},{10,9},{11,1... | collective-permute-start | bytes 786440 | tf_op jit(solution)/shard_map/ppermute | solution.py:173
  26.0 14.7 %collective-permute-start.6 = (f32[2,128,256]{2,1,0:T(8,128)S(1)}, f32[2,128,256]{2,1,0:T(8,128)S(1)}, u32[]{:S(2)}, u32[]{:S(2)}) collective-permute-start(f32[2,128,256]{2,1,0:T(8,128)S(1)} %get-tuple-element.22), channel_id=1, source_target_pairs={{1,16},{2,17},{3,18},{4,19},{5,20},{6,21},{7,22},{8,23},{9,24},{10... | collective-permute-start | bytes 786440 | tf_op jit(solution)/shard_map/ppermute | solution.py:174
  40.7 2.2 %copy-start.1 = (bf16[4,2,512,512]{3,2,1,0:T(8,128)(2,1)S(1)}, bf16[4,2,512,512]{3,2,1,0:T(8,128)(2,1)}, u32[]{:S(2)}) copy-start(bf16[4,2,512,512]{3,2,1,0:T(8,128)(2,1)} %constant.25.clone.table) | copy-start | bytes 12582916
  49.4 13.0 %collective-permute-start.7 = (f32[2,128,256]{2,1,0:T(8,128)S(1)}, f32[2,128,256]{2,1,0:T(8,128)S(1)}, u32[]{:S(2)}, u32[]{:S(2)}) collective-permute-start(f32[2,128,256]{2,1,0:T(8,128)S(1)} %get-tuple-element.23), channel_id=1, source_target_pairs={{0,1},{1,2},{2,3},{3,4},{4,5},{5,6},{6,7},{7,8},{8,9},{9,10},{10,1... | collective-permute-start | bytes 786440 | tf_op jit(solution)/shard_map/ppermute | solution.py:169
  51.3 14.8 %collective-permute-start.8 = (f32[2,128,256]{2,1,0:T(8,128)S(1)}, f32[2,128,256]{2,1,0:T(8,128)S(1)}, u32[]{:S(2)}, u32[]{:S(2)}) collective-permute-start(f32[2,128,256]{2,1,0:T(8,128)S(1)} %get-tuple-element.24), channel_id=1, source_target_pairs={{0,17},{1,18},{2,19},{3,20},{4,21},{5,22},{6,23},{7,24},{8,25},{9,... | collective-permute-start | bytes 786440 | tf_op jit(solution)/shard_map/ppermute | solution.py:170
  58.1 8.0 %collective-permute-start.9 = (f32[2,128,256]{2,1,0:T(8,128)S(1)}, f32[2,128,256]{2,1,0:T(8,128)S(1)}, u32[]{:S(2)}, u32[]{:S(2)}) collective-permute-start(f32[2,128,256]{2,1,0:T(8,128)S(1)} %get-tuple-element.26), channel_id=1, source_target_pairs={{0,16},{16,0},{1,17},{17,1},{2,18},{18,2},{3,19},{19,3},{4,20},{20... | collective-permute-start | bytes 786440 | tf_op jit(solution)/shard_map/ppermute | solution.py:172
  58.2 14.7 %collective-permute-start.10 = (f32[2,128,256]{2,1,0:T(8,128)S(1)}, f32[2,128,256]{2,1,0:T(8,128)S(1)}, u32[]{:S(2)}, u32[]{:S(2)}) collective-permute-start(f32[2,128,256]{2,1,0:T(8,128)S(1)} %get-tuple-element.27), channel_id=1, source_target_pairs={{1,0},{2,1},{3,2},{4,3},{5,4},{6,5},{7,6},{8,7},{9,8},{10,9},{11,1... | collective-permute-start | bytes 786440 | tf_op jit(solution)/shard_map/ppermute | solution.py:173
  60.1 18.9 %collective-permute-start.11 = (f32[2,128,256]{2,1,0:T(8,128)S(1)}, f32[2,128,256]{2,1,0:T(8,128)S(1)}, u32[]{:S(2)}, u32[]{:S(2)}) collective-permute-start(f32[2,128,256]{2,1,0:T(8,128)S(1)} %get-tuple-element.28), channel_id=1, source_target_pairs={{1,16},{2,17},{3,18},{4,19},{5,20},{6,21},{7,22},{8,23},{9,24},{10... | collective-permute-start | bytes 786440 | tf_op jit(solution)/shard_map/ppermute | solution.py:174
